TPU v7x, 512 devices: a whole 4x4x16 slice. The times are simulated.
512 devices in a mesh: grp: 16 (over x, y), dev: 32 (over z, core).
Axes of the slice: x: 4, y: 4, z: 16, core: 2. Of those that a mesh axis runs over, the one named last changes fastest.
Arguments:
- block_vectors: float32 [262144, 64], P(('grp', 'dev')), may hold values from -6 to 6
- hamiltonian: float32 [4096, 64, 2048], P(('grp', 'dev')), may hold values from -0.125 to 0.125
- pattern: int32 [4096, 32], P(('grp', 'dev')), may hold values from 0 to 4095, as said below
- owned_blocks: int32 [512], P(('grp', 'dev')), may hold values from 1 to 8, as said below
- spectrum: float32 [2], replicated, may hold values from 0.5 to 2
Outputs:
- basis: float32 [262144, 64], P(('grp', 'dev'))
- r_factor: float32 [64, 64], replicated
Inputs may be any that keep to these rules, and one draw needn't show every extreme that they name: pattern[b, 0] = b; every other entry is b + o clipped to the slots, for a distinct nonzero o with |o| <= 16. `owned_blocks`: some device owns all 8 slots.
All inputs are finite; a program needn't handle non-finite values.
Results may differ from a plain program's by a relative error of at most 0.0003.
Values sent between devices are 32-bit elements; how exact they have to be, the bound alone decides.
A program may use at most 64 MiB of HBM per device.

v0:
```python
import jax
import jax.numpy as jnp
from jax import lax
from jax.sharding import PartitionSpec as P

BAND = 16


def shifted(block, axis, distance):
    devices = range(lax.axis_size(axis))
    route = [(i - distance, i) for i in devices if i - distance in devices]
    return lax.ppermute(block, axis, route)


def send_direct(values, distance):
    return shifted(values, ("grp", "dev"), distance)


def extend_band(values, reach_dev):
    lowers = []
    uppers = []
    for distance in range(reach_dev, 0, -1):
        lowers.append(send_direct(values, distance))
    for distance in range(1, reach_dev + 1):
        uppers.append(send_direct(values, -distance))
    return jnp.concatenate(lowers + [values] + uppers, axis=0)


def apply_matrix(values, hamiltonian, local_index, reach_dev):
    extended = extend_band(values, reach_dev)
    block_count, neighbours = local_index.shape
    picked = jnp.take(extended, local_index, axis=0)
    picked = picked.reshape(block_count, neighbours * values.shape[1], values.shape[2])
    return jnp.einsum("gik,gkc->gic", hamiltonian, picked, precision=lax.Precision.HIGHEST)


def summed_gram(flat):
    local_gram = jnp.dot(
        flat.T, flat, precision=lax.Precision.HIGHEST, preferred_element_type=jnp.float32
    )
    return lax.psum(local_gram, ("grp", "dev"))


def cholesky_step(flat):
    gram_total = summed_gram(flat)
    upper = jnp.linalg.cholesky(gram_total).T
    ortho = jax.scipy.linalg.solve_triangular(upper.T, flat.T, lower=True).T
    return (ortho, upper)


def on_device(block_vectors, hamiltonian, pattern, owned_blocks, spectrum):
    block_count = pattern.shape[0]
    block_size = hamiltonian.shape[1]
    columns = block_vectors.shape[1]
    reach_dev = (BAND + block_count - 1) // block_count
    first_block = lax.axis_index(("grp", "dev")) * block_count
    local_index = pattern - first_block + reach_dev * block_count
    live_mask = (jnp.arange(block_count, dtype=jnp.int32) < owned_blocks[0]).astype(jnp.float32)[
        :, None, None
    ]
    shift_value = spectrum[0]
    scale_value = spectrum[1]
    first_vec = block_vectors.reshape(block_count, block_size, columns) * live_mask
    second_vec = live_mask * (
        (apply_matrix(first_vec, hamiltonian, local_index, reach_dev) - shift_value * first_vec)
        / scale_value
    )
    third_vec = live_mask * (
        2.0
        * (apply_matrix(second_vec, hamiltonian, local_index, reach_dev) - shift_value * second_vec)
        / scale_value
        - first_vec
    )
    flat = third_vec.reshape(block_count * block_size, columns)
    ortho_one, upper_one = cholesky_step(flat)
    ortho_two, upper_two = cholesky_step(ortho_one)
    upper_all = jnp.dot(
        upper_two, upper_one, precision=lax.Precision.HIGHEST, preferred_element_type=jnp.float32
    )
    total = jnp.sqrt(
        jnp.float32(block_count * block_size * lax.axis_size("grp") * lax.axis_size("dev"))
    )
    return (ortho_two * total, upper_all / total)


def solution(mesh):
    placed = (
        P(("grp", "dev"), None),
        P(("grp", "dev"), None, None),
        P(("grp", "dev"), None),
        P(("grp", "dev")),
        P(),
    )
    return jax.shard_map(
        on_device,
        mesh=mesh,
        in_specs=placed,
        out_specs=(P(("grp", "dev"), None), P()),
        check_vma=False,
    )
```

profile of v0, /device:TPU:1, one launch (start us, length us, event | category | flops | bytes accessed | tf_op | source)
XLA Modules:
  0.0 355.4 jit_solution(15956783039810358615)
XLA Ops:
  1.3 1.0 reshape.34
  2.3 0.1 copy_multiply_fusion
  2.4 1.3 collective-permute-start.3
  3.7 8.8 %collective-permute-start.2 = (f32[8,64,64]{1,2,0:T(8,128)S(1)}, f32[8,64,64]{1,2,0:T(8,128)S(1)}, u32[]{:S(2)}, u32[]{:S(2)}) collective-permute-start(f32[8,64,64]{1,2,0:T(8,128)S(1)} %copy_multiply_fusion), channel_id=1, source_target_pairs={{1,0},{2,1},{3,2},{4,3},{5,4},{6,5},{7,6},{8,7},{9,8},{10,9},{11,1... | collective-permute-start | bytes 393224 | tf_op jit(solution)/shard_map/ppermute | solution.py:12
  12.5 4.2 %collective-permute-start.1 = (f32[8,64,64]{1,2,0:T(8,128)S(1)}, f32[8,64,64]{1,2,0:T(8,128)S(1)}, u32[]{:S(2)}, u32[]{:S(2)}) collective-permute-start(f32[8,64,64]{1,2,0:T(8,128)S(1)} %copy_multiply_fusion), channel_id=1, source_target_pairs={{0,1},{1,2},{2,3},{3,4},{4,5},{5,6},{6,7},{7,8},{8,9},{9,10},{10,1... | collective-permute-start | bytes 393224 | tf_op jit(solution)/shard_map/ppermute | solution.py:12
  16.7 2.0 collective-permute-start
  18.7 0.7 compare_and_fusion
  19.4 1.3 fusion.29
  20.7 0.1 reshape.58
  20.8 4.5 %collective-permute-done = f32[8,64,64]{1,2,0:T(8,128)S(1)} collective-permute-done((f32[8,64,64]{1,2,0:T(8,128)S(1)}, f32[8,64,64]{1,2,0:T(8,128)S(1)}, u32[]{:S(2)}, u32[]{:S(2)}) %collective-permute-start) | collective-permute-done | bytes 131104 | tf_op jit(solution)/shard_map/ppermute | solution.py:12
  25.4 0.1 constant_dynamic-update-slice_fusion.2
  25.6 4.4 %gather_fusion = f32[256,64,64]{1,2,0:T(8,128)} fusion(f32[40,64,64]{1,2,0:T(8,128)S(1)} %constant_dynamic-update-slice_fusion, s32[1024]{0:T(1024)S(1)} %pad_clamp_fusion), kind=kCustom, calls=%fused_computation.clone | custom fusion | bytes 8389632 | tf_op jit(solution)/shard_map/jit(_take)/gather | solution.py:32
  29.9 3.8 %broadcast_select_fusion.1 = f32[8,32,64,64]{2,3,1,0:T(8,128)S(1)} fusion(f32[8,32,64,64]{2,3,1,0:T(8,128)} %bitcast.73, pred[8,32]{1,0:T(8,128)(4,1)S(1)} %get-tuple-element.4), kind=kLoop, calls=%fused_computation.3 | loop fusion | flops 1048576 | bytes 8388864 | tf_op jit(solution)/shard_map/jit(_take)/select_n | solution.py:32
  33.8 8.0 %copy.15 = f32[8,32,64,64]{2,1,3,0:T(8,128)} copy(f32[8,32,64,64]{2,3,1,0:T(8,128)S(1)} %broadcast_select_fusion.1) | data formatting | bytes 8388608 | tf_op jit(solution)/shard_map/jit(_take)/select_n | solution.py:32
  41.8 7.8 %reshape.35 = f32[8,2048,64]{1,2,0:T(8,128)} reshape(f32[8,32,64,64]{2,1,3,0:T(8,128)} %copy.15) | data formatting | bytes 8388608 | tf_op jit(solution)/shard_map/reshape | solution.py:33
  49.6 8.7 %fusion.4 = f32[8,64,64]{1,2,0:T(8,128)S(1)} fusion(f32[8,2048,64]{1,2,0:T(8,128)} %reshape.35, f32[8,64,2048]{2,1,0:T(8,128)} %param.11, f32[]{:T(128)} %bitcast.4, f32[]{:T(128)} %bitcast.3, f32[8]{0:T(128)S(1)} %compare_convert_fusion, f32[8,64,64]{1,0,2:T(8,128)S(1)} %reshape.34), kind=kOutput, calls=%fused_computation.10 | convolution fusion | flops 805470208 | bytes 8650792 | tf_op jit(solution)/shard_map/gik,gkc->gic/dot_general | solution.py:34
  58.3 4.1 %collective-permute-start.4 = (f32[8,64,64]{1,2,0:T(8,128)S(1)}, f32[8,64,64]{1,2,0:T(8,128)S(1)}, u32[]{:S(2)}, u32[]{:S(2)}) collective-permute-start(f32[8,64,64]{1,2,0:T(8,128)S(1)} %fusion.4), channel_id=1, source_target_pairs={{0,2},{1,3},{2,4},{3,5},{4,6},{5,7},{6,8},{7,9},{8,10},{9,11},{10,... | collective-permute-start | bytes 393224 | tf_op jit(solution)/shard_map/ppermute | solution.py:12
  62.4 2.7 collective-permute-start.5
  65.1 1.3 collective-permute-start.7
  66.4 2.1 collective-permute-start.6
  68.5 0.0 collective-permute-done.4
  68.5 2.8 collective-permute-done.5
  71.3 6.5 %collective-permute-done.6 = f32[8,64,64]{1,2,0:T(8,128)S(1)} collective-permute-done((f32[8,64,64]{1,2,0:T(8,128)S(1)}, f32[8,64,64]{1,2,0:T(8,128)S(1)}, u32[]{:S(2)}, u32[]{:S(2)}) %collective-permute-start.6) | collective-permute-done | bytes 131104 | tf_op jit(solution)/shard_map/ppermute | solution.py:12
  77.8 0.0 collective-permute-done.7
  77.9 4.4 %gather_fusion.1 = f32[256,64,64]{1,2,0:T(8,128)} fusion(f32[40,64,64]{1,2,0:T(8,128)S(1)} %constant_dynamic-update-slice_fusion.5, s32[1024]{0:T(1024)S(1)} %pad_clamp_fusion), kind=kCustom, calls=%fused_computation.1.clone | custom fusion | bytes 8389632 | tf_op jit(solution)/shard_map/jit(_take)/gather | solution.py:32
  82.2 3.8 %broadcast_select_fusion = f32[8,32,64,64]{2,3,1,0:T(8,128)S(1)} fusion(f32[8,32,64,64]{2,3,1,0:T(8,128)} %bitcast.72, pred[8,32]{1,0:T(8,128)(4,1)S(1)} %get-tuple-element.4), kind=kLoop, calls=%fused_computation.2 | loop fusion | flops 1048576 | bytes 8388864 | tf_op jit(solution)/shard_map/jit(_take)/select_n | solution.py:32
  86.1 8.0 %copy.16 = f32[8,32,64,64]{2,1,3,0:T(8,128)} copy(f32[8,32,64,64]{2,3,1,0:T(8,128)S(1)} %broadcast_select_fusion) | data formatting | bytes 8388608 | tf_op jit(solution)/shard_map/jit(_take)/select_n | solution.py:32
  94.1 7.8 %reshape.36 = f32[8,2048,64]{1,2,0:T(8,128)} reshape(f32[8,32,64,64]{2,1,3,0:T(8,128)} %copy.16) | data formatting | bytes 8388608 | tf_op jit(solution)/shard_map/reshape | solution.py:33
  101.9 8.7 %fusion.7 = f32[8,64,64]{1,2,0:T(8,128)S(1)} fusion(f32[8,2048,64]{1,2,0:T(8,128)} %reshape.36, f32[8,64,2048]{2,1,0:T(8,128)} %param.11, f32[8,64,64]{1,2,0:T(8,128)S(1)} %fusion.4, f32[]{:T(128)} %bitcast.4, f32[]{:T(128)} %bitcast.3, f32[8]{0:T(128)S(1)} %compare_convert_fusion, f32[8,64,64]{1,0,2:T(8,128)S(1)} %reshape.34), kind=kOutput, calls=%fused_computation.13 | convolution fusion | flops 805535744 | bytes 8781864 | tf_op jit(solution)/shard_map/gik,gkc->gic/dot_general | solution.py:34
  110.6 0.4 convolution_bitcast_fusion.2
  111.0 0.2 copy.20
  111.1 116.5 %psum.14 = f32[64,64]{0,1:T(8,128)S(1)} all-reduce(f32[64,64]{0,1:T(8,128)S(1)} %convolution_bitcast_fusion.2), channel_id=1, replica_groups=mesh['grp'=16,'dev'=32] {'grp','dev'}, use_global_device_ids=true, to_apply=%region_0.0 | all-reduce | flops 4096 | bytes 32768 | tf_op jit(solution)/shard_map/psum | solution.py:41
  227.7 0.1 reshape.37
  227.8 0.1 copy.19
  227.9 5.8 %cholesky.44 = f32[64,64]{1,0:T(8,128)S(1)} custom-call(f32[64,64]{1,0:T(8,128)S(1)} %fusion.14), custom_call_target="Cholesky" | custom-call | tf_op jit(solution)/shard_map/jit(cholesky)/cholesky | solution.py:46
  233.8 0.6 compare_reduce_fusion.1
  234.4 0.7 fusion.18
  235.1 4.9 %custom-call.6 = f32[1,64,64]{1,2,0:T(8,128)S(1)} custom-call(f32[1,64,64]{2,1,0:T(8,128)S(1)} %fusion.18), custom_call_target="InvertDiagBlocksLowerTriangular" | custom-call | tf_op jit(solution)/shard_map/jit(_solve_triangular)/triangular_solve | solution.py:47
  240.0 0.3 fusion.9
  240.3 0.3 fusion.30
  240.6 99.3 %psum.15 = f32[64,64]{0,1:T(8,128)S(1)} all-reduce(f32[64,64]{0,1:T(8,128)S(1)} %fusion.30), channel_id=1, replica_groups=mesh['grp'=16,'dev'=32] {'grp','dev'}, use_global_device_ids=true, to_apply=%region_3.7 | all-reduce | flops 4096 | bytes 32768 | tf_op jit(solution)/shard_map/psum | solution.py:41
  339.9 0.1 copy.22
  340.0 5.8 %cholesky.55 = f32[64,64]{1,0:T(8,128)S(1)} custom-call(f32[64,64]{1,0:T(8,128)S(1)} %fusion.12), custom_call_target="Cholesky" | custom-call | tf_op jit(solution)/shard_map/jit(cholesky)/cholesky | solution.py:46
  345.9 0.7 compare_reduce_fusion
  346.6 2.2 convolution_multiply_fusion.1
  348.8 0.7 select_bitcast_fusion
  349.5 4.9 %custom-call.7 = f32[1,64,64]{1,2,0:T(8,128)S(1)} custom-call(f32[1,64,64]{2,1,0:T(8,128)S(1)} %select_bitcast_fusion), custom_call_target="InvertDiagBlocksLowerTriangular" | custom-call | tf_op jit(solution)/shard_map/jit(_solve_triangular)/triangular_solve | solution.py:47
  354.4 1.0 fusion.8
  (18 shorter events, 0.3 us)
Async XLA Ops:
  2.4 23.1 %collective-permute-start.3 = (f32[8,64,64]{1,2,0:T(8,128)S(1)}, f32[8,64,64]{1,2,0:T(8,128)S(1)}, u32[]{:S(2)}, u32[]{:S(2)}) collective-permute-start(f32[8,64,64]{1,2,0:T(8,128)S(1)} %copy_multiply_fusion), channel_id=1, source_target_pairs={{2,0},{3,1},{4,2},{5,3},{6,4},{7,5},{8,6},{9,7},{10,8},{11,9},{12,... | collective-permute-start | bytes 393224 | tf_op jit(solution)/shard_map/ppermute | solution.py:12
  3.7 21.8 %collective-permute-start.2 = (f32[8,64,64]{1,2,0:T(8,128)S(1)}, f32[8,64,64]{1,2,0:T(8,128)S(1)}, u32[]{:S(2)}, u32[]{:S(2)}) collective-permute-start(f32[8,64,64]{1,2,0:T(8,128)S(1)} %copy_multiply_fusion), channel_id=1, source_target_pairs={{1,0},{2,1},{3,2},{4,3},{5,4},{6,5},{7,6},{8,7},{9,8},{10,9},{11,1... | collective-permute-start | bytes 393224 | tf_op jit(solution)/shard_map/ppermute | solution.py:12
  12.5 12.9 %collective-permute-start.1 = (f32[8,64,64]{1,2,0:T(8,128)S(1)}, f32[8,64,64]{1,2,0:T(8,128)S(1)}, u32[]{:S(2)}, u32[]{:S(2)}) collective-permute-start(f32[8,64,64]{1,2,0:T(8,128)S(1)} %copy_multiply_fusion), channel_id=1, source_target_pairs={{0,1},{1,2},{2,3},{3,4},{4,5},{5,6},{6,7},{7,8},{8,9},{9,10},{10,1... | collective-permute-start | bytes 393224 | tf_op jit(solution)/shard_map/ppermute | solution.py:12
  16.7 8.7 %collective-permute-start = (f32[8,64,64]{1,2,0:T(8,128)S(1)}, f32[8,64,64]{1,2,0:T(8,128)S(1)}, u32[]{:S(2)}, u32[]{:S(2)}) collective-permute-start(f32[8,64,64]{1,2,0:T(8,128)S(1)} %copy_multiply_fusion), channel_id=1, source_target_pairs={{0,2},{1,3},{2,4},{3,5},{4,6},{5,7},{6,8},{7,9},{8,10},{9,11},{10,... | collective-permute-start | bytes 393224 | tf_op jit(solution)/shard_map/ppermute | solution.py:12
  58.3 10.2 %collective-permute-start.4 = (f32[8,64,64]{1,2,0:T(8,128)S(1)}, f32[8,64,64]{1,2,0:T(8,128)S(1)}, u32[]{:S(2)}, u32[]{:S(2)}) collective-permute-start(f32[8,64,64]{1,2,0:T(8,128)S(1)} %fusion.4), channel_id=1, source_target_pairs={{0,2},{1,3},{2,4},{3,5},{4,6},{5,7},{6,8},{7,9},{8,10},{9,11},{10,... | collective-permute-start | bytes 393224 | tf_op jit(solution)/shard_map/ppermute | solution.py:12
  62.4 8.9 %collective-permute-start.5 = (f32[8,64,64]{1,2,0:T(8,128)S(1)}, f32[8,64,64]{1,2,0:T(8,128)S(1)}, u32[]{:S(2)}, u32[]{:S(2)}) collective-permute-start(f32[8,64,64]{1,2,0:T(8,128)S(1)} %fusion.4), channel_id=1, source_target_pairs={{0,1},{1,2},{2,3},{3,4},{4,5},{5,6},{6,7},{7,8},{8,9},{9,10},{10,1... | collective-permute-start | bytes 393224 | tf_op jit(solution)/shard_map/ppermute | solution.py:12
  65.1 12.8 %collective-permute-start.7 = (f32[8,64,64]{1,2,0:T(8,128)S(1)}, f32[8,64,64]{1,2,0:T(8,128)S(1)}, u32[]{:S(2)}, u32[]{:S(2)}) collective-permute-start(f32[8,64,64]{1,2,0:T(8,128)S(1)} %fusion.4), channel_id=1, source_target_pairs={{2,0},{3,1},{4,2},{5,3},{6,4},{7,5},{8,6},{9,7},{10,8},{11,9},{12,... | collective-permute-start | bytes 393224 | tf_op jit(solution)/shard_map/ppermute | solution.py:12
  66.4 11.4 %collective-permute-start.6 = (f32[8,64,64]{1,2,0:T(8,128)S(1)}, f32[8,64,64]{1,2,0:T(8,128)S(1)}, u32[]{:S(2)}, u32[]{:S(2)}) collective-permute-start(f32[8,64,64]{1,2,0:T(8,128)S(1)} %fusion.4), channel_id=1, source_target_pairs={{1,0},{2,1},{3,2},{4,3},{5,4},{6,5},{7,6},{8,7},{9,8},{10,9},{11,1... | collective-permute-start | bytes 393224 | tf_op jit(solution)/shard_map/ppermute | solution.py:12
where the time goes:
time: 356 us; the launch traced here: 355 us
  blocking collectives  216 us (61%)
  local copies, waits for them, and re-layouts  43.3 us (12%)
  other arithmetic  32.9 us (9%)
  starting transfers between devices  26.5 us (7%)
  matrix products  21.5 us (6%)
  waiting for transfers between devices  13.8 us (4%)
    psum x2, blocking collectives, summed_gram(): return lax.psum(local_gram, ('grp', 'dev'))  216 us
    ppermute x8, starting transfers between devices, shifted(): return lax.ppermute(block, axis, route)  26.5 us
    dot_general x2, matrix products, apply_matrix(): jnp.einsum('gik,gkc->gic', hamiltonian, picked, precision=lax.Precision.H...  17.4 us
    select_n x2, local copies, waits for them, and re-layouts, apply_matrix(): picked = jnp.take(extended, local_index, axis=0)  16 us
    reshape x2, local copies, waits for them, and re-layouts, apply_matrix(): picked.reshape(block_count, neighbours * values.shape[1], values.shape[2])  15.6 us
    ppermute x8, waiting for transfers between devices, shifted(): return lax.ppermute(block, axis, route)  13.8 us
    another operation x6, other arithmetic, cholesky_step(): upper = jnp.linalg.cholesky(gram_total).T  13.1 us
    another operation x4, other arithmetic, cholesky_step(): ortho = jax.scipy.linalg.solve_triangular(upper.T, flat.T, lower=True).T  11.1 us
  transfers between devices with their start and end apart: 8, of which 3 were waited for; matrix products, arithmetic and copies ran while one was open for 1% of the time, Pallas kernels for 0%

commit v1 on v0

--- a/solution.py
+++ b/solution.py
@@ -4,6 +4,11 @@
 from jax.sharding import PartitionSpec as P
 
 BAND = 16
+
+
+def show_the_shifts_all(field):
+    now = lax.psum(lax.psum(field, axis_name="dev"), "grp")
+    return now
 
 
 def shifted(block, axis, distance):
@@ -38,7 +43,7 @@
     local_gram = jnp.dot(
         flat.T, flat, precision=lax.Precision.HIGHEST, preferred_element_type=jnp.float32
     )
-    return lax.psum(local_gram, ("grp", "dev"))
+    return show_the_shifts_all(local_gram)
 
 
 def cholesky_step(flat):

time: 356 us -> 471 us (1.32)
  the two profiles are of different devices: /device:TPU:1 before, /device:TPU:8 now
where the time goes in v1:
time: 471 us; the launch traced here: 470 us
  blocking collectives  326 us (69%)
  local copies, waits for them, and re-layouts  43.3 us (9%)
  other arithmetic  32.9 us (7%)
  starting transfers between devices  31.6 us (7%)
  matrix products  21.5 us (5%)
  waiting for transfers between devices  13.5 us (3%)
    psum x4, blocking collectives, show_the_shifts_all(): now = lax.psum(lax.psum(field, axis_name='dev'), 'grp')  326 us
    ppermute x8, starting transfers between devices, shifted(): return lax.ppermute(block, axis, route)  31.6 us
    dot_general x2, matrix products, apply_matrix(): jnp.einsum('gik,gkc->gic', hamiltonian, picked, precision=lax.Precision.H...  17.4 us
    select_n x2, local copies, waits for them, and re-layouts, apply_matrix(): picked = jnp.take(extended, local_index, axis=0)  16 us
    reshape x2, local copies, waits for them, and re-layouts, apply_matrix(): picked.reshape(block_count, neighbours * values.shape[1], values.shape[2])  15.6 us
    ppermute x8, waiting for transfers between devices, shifted(): return lax.ppermute(block, axis, route)  13.5 us
    another operation x6, other arithmetic, cholesky_step(): upper = jnp.linalg.cholesky(gram_total).T  13.1 us
    another operation x4, other arithmetic, cholesky_step(): ortho = jax.scipy.linalg.solve_triangular(upper.T, flat.T, lower=True).T  11.1 us
  transfers between devices with their start and end apart: 8, of which 3 were waited for; matrix products, arithmetic and copies ran while one was open for 0% of the time, Pallas kernels for 0%

profile of v1, /device:TPU:8, one launch (start us, length us, event | category | flops | bytes accessed | tf_op | source)
XLA Modules:
  0.0 470.2 jit_solution(5157332896381841652)
XLA Ops:
  1.3 1.0 reshape.34
  2.3 0.1 copy_multiply_fusion
  2.4 11.3 %collective-permute-start.3 = (f32[8,64,64]{1,2,0:T(8,128)S(1)}, f32[8,64,64]{1,2,0:T(8,128)S(1)}, u32[]{:S(2)}, u32[]{:S(2)}) collective-permute-start(f32[8,64,64]{1,2,0:T(8,128)S(1)} %copy_multiply_fusion), channel_id=1, source_target_pairs={{2,0},{3,1},{4,2},{5,3},{6,4},{7,5},{8,6},{9,7},{10,8},{11,9},{12,... | collective-permute-start | bytes 393224 | tf_op jit(solution)/shard_map/ppermute | solution.py:17
  13.7 2.1 collective-permute-start.2
  15.8 2.3 collective-permute-start.1
  18.0 2.6 collective-permute-start
  20.6 0.7 compare_and_fusion
  21.3 1.3 fusion.29
  22.7 0.1 reshape.58
  22.7 8.5 %collective-permute-done = f32[8,64,64]{1,2,0:T(8,128)S(1)} collective-permute-done((f32[8,64,64]{1,2,0:T(8,128)S(1)}, f32[8,64,64]{1,2,0:T(8,128)S(1)}, u32[]{:S(2)}, u32[]{:S(2)}) %collective-permute-start) | collective-permute-done | bytes 131104 | tf_op jit(solution)/shard_map/ppermute | solution.py:17
  31.2 0.1 constant_dynamic-update-slice_fusion.2
  31.4 4.4 gather_fusion
  35.8 3.8 broadcast_select_fusion.1
  39.6 8.0 %copy.15 = f32[8,32,64,64]{2,1,3,0:T(8,128)} copy(f32[8,32,64,64]{2,3,1,0:T(8,128)S(1)} %broadcast_select_fusion.1) | data formatting | bytes 8388608 | tf_op jit(solution)/shard_map/jit(_take)/select_n | solution.py:37
  47.6 7.8 %reshape.35 = f32[8,2048,64]{1,2,0:T(8,128)} reshape(f32[8,32,64,64]{2,1,3,0:T(8,128)} %copy.15) | data formatting | bytes 8388608 | tf_op jit(solution)/shard_map/reshape | solution.py:38
  55.4 8.7 %fusion.4 = f32[8,64,64]{1,2,0:T(8,128)S(1)} fusion(f32[8,2048,64]{1,2,0:T(8,128)} %reshape.35, f32[8,64,2048]{2,1,0:T(8,128)} %param.11, f32[]{:T(128)} %bitcast.4, f32[]{:T(128)} %bitcast.3, f32[8]{0:T(128)S(1)} %compare_convert_fusion, f32[8,64,64]{1,0,2:T(8,128)S(1)} %reshape.34), kind=kOutput, calls=%fused_computation.10 | convolution fusion | flops 805470208 | bytes 8650792 | tf_op jit(solution)/shard_map/gik,gkc->gic/dot_general | solution.py:39
  64.1 1.9 collective-permute-start.4
  66.1 1.9 collective-permute-start.5
  68.0 6.0 %collective-permute-start.7 = (f32[8,64,64]{1,2,0:T(8,128)S(1)}, f32[8,64,64]{1,2,0:T(8,128)S(1)}, u32[]{:S(2)}, u32[]{:S(2)}) collective-permute-start(f32[8,64,64]{1,2,0:T(8,128)S(1)} %fusion.4), channel_id=1, source_target_pairs={{2,0},{3,1},{4,2},{5,3},{6,4},{7,5},{8,6},{9,7},{10,8},{11,9},{12,... | collective-permute-start | bytes 393224 | tf_op jit(solution)/shard_map/ppermute | solution.py:17
  74.0 3.5 collective-permute-start.6
  77.6 1.6 collective-permute-done.5
  79.2 3.4 collective-permute-done.6
  82.7 4.4 gather_fusion.1
  87.1 3.8 broadcast_select_fusion
  90.9 8.0 %copy.16 = f32[8,32,64,64]{2,1,3,0:T(8,128)} copy(f32[8,32,64,64]{2,3,1,0:T(8,128)S(1)} %broadcast_select_fusion) | data formatting | bytes 8388608 | tf_op jit(solution)/shard_map/jit(_take)/select_n | solution.py:37
  98.9 7.8 %reshape.36 = f32[8,2048,64]{1,2,0:T(8,128)} reshape(f32[8,32,64,64]{2,1,3,0:T(8,128)} %copy.16) | data formatting | bytes 8388608 | tf_op jit(solution)/shard_map/reshape | solution.py:38
  106.7 8.7 %fusion.7 = f32[8,64,64]{1,2,0:T(8,128)S(1)} fusion(f32[8,2048,64]{1,2,0:T(8,128)} %reshape.36, f32[8,64,2048]{2,1,0:T(8,128)} %param.11, f32[8,64,64]{1,2,0:T(8,128)S(1)} %fusion.4, f32[]{:T(128)} %bitcast.4, f32[]{:T(128)} %bitcast.3, f32[8]{0:T(128)S(1)} %compare_convert_fusion, f32[8,64,64]{1,0,2:T(8,128)S(1)} %reshape.34), kind=kOutput, calls=%fused_computation.13 | convolution fusion | flops 805535744 | bytes 8781864 | tf_op jit(solution)/shard_map/gik,gkc->gic/dot_general | solution.py:39
  115.4 0.4 convolution_bitcast_fusion.2
  115.8 0.2 copy.20
  116.0 0.1 reshape.37
  116.1 94.1 %psum.28 = f32[64,64]{0,1:T(8,128)S(1)} all-reduce(f32[64,64]{0,1:T(8,128)S(1)} %convolution_bitcast_fusion.2), channel_id=1, replica_groups=mesh['grp'=16,'dev'=32] {'dev'}, use_global_device_ids=true, to_apply=%region_0.0 | all-reduce | flops 4096 | bytes 32768 | tf_op jit(solution)/shard_map/psum | solution.py:10
  210.2 70.1 %psum.29 = f32[64,64]{0,1:T(8,128)S(1)} all-reduce(f32[64,64]{0,1:T(8,128)S(1)} %psum.28), channel_id=1, replica_groups=mesh['grp'=16,'dev'=32] {'grp'}, use_global_device_ids=true, to_apply=%region_1.3 | all-reduce | flops 4096 | bytes 32768 | tf_op jit(solution)/shard_map/psum | solution.py:10
  280.3 0.1 copy.19
  280.4 5.8 %cholesky.44 = f32[64,64]{1,0:T(8,128)S(1)} custom-call(f32[64,64]{1,0:T(8,128)S(1)} %fusion.14), custom_call_target="Cholesky" | custom-call | tf_op jit(solution)/shard_map/jit(cholesky)/cholesky | solution.py:51
  286.2 0.6 compare_reduce_fusion.1
  286.9 0.7 fusion.18
  287.6 4.9 %custom-call.6 = f32[1,64,64]{1,2,0:T(8,128)S(1)} custom-call(f32[1,64,64]{2,1,0:T(8,128)S(1)} %fusion.18), custom_call_target="InvertDiagBlocksLowerTriangular" | custom-call | tf_op jit(solution)/shard_map/jit(_solve_triangular)/triangular_solve | solution.py:52
  292.4 0.3 fusion.9
  292.8 0.3 fusion.30
  293.1 90.0 %psum.30 = f32[64,64]{0,1:T(8,128)S(1)} all-reduce(f32[64,64]{0,1:T(8,128)S(1)} %fusion.30), channel_id=1, replica_groups=mesh['grp'=16,'dev'=32] {'dev'}, use_global_device_ids=true, to_apply=%region_4.8 | all-reduce | flops 4096 | bytes 32768 | tf_op jit(solution)/shard_map/psum | solution.py:10
  383.1 71.7 %psum.31 = f32[64,64]{0,1:T(8,128)S(1)} all-reduce(f32[64,64]{0,1:T(8,128)S(1)} %psum.30), channel_id=1, replica_groups=mesh['grp'=16,'dev'=32] {'grp'}, use_global_device_ids=true, to_apply=%region_5.9 | all-reduce | flops 4096 | bytes 32768 | tf_op jit(solution)/shard_map/psum | solution.py:10
  454.7 0.1 copy.22
  454.8 5.8 %cholesky.55 = f32[64,64]{1,0:T(8,128)S(1)} custom-call(f32[64,64]{1,0:T(8,128)S(1)} %fusion.12), custom_call_target="Cholesky" | custom-call | tf_op jit(solution)/shard_map/jit(cholesky)/cholesky | solution.py:51
  460.7 0.7 compare_reduce_fusion
  461.4 2.2 convolution_multiply_fusion.1
  463.6 0.7 select_bitcast_fusion
  464.3 4.9 %custom-call.7 = f32[1,64,64]{1,2,0:T(8,128)S(1)} custom-call(f32[1,64,64]{2,1,0:T(8,128)S(1)} %select_bitcast_fusion), custom_call_target="InvertDiagBlocksLowerTriangular" | custom-call | tf_op jit(solution)/shard_map/jit(_solve_triangular)/triangular_solve | solution.py:52
  469.2 1.0 fusion.8
  (20 shorter events, 0.3 us)
Async XLA Ops:
  2.4 29.0 %collective-permute-start.3 = (f32[8,64,64]{1,2,0:T(8,128)S(1)}, f32[8,64,64]{1,2,0:T(8,128)S(1)}, u32[]{:S(2)}, u32[]{:S(2)}) collective-permute-start(f32[8,64,64]{1,2,0:T(8,128)S(1)} %copy_multiply_fusion), channel_id=1, source_target_pairs={{2,0},{3,1},{4,2},{5,3},{6,4},{7,5},{8,6},{9,7},{10,8},{11,9},{12,... | collective-permute-start | bytes 393224 | tf_op jit(solution)/shard_map/ppermute | solution.py:17
  13.7 17.7 %collective-permute-start.2 = (f32[8,64,64]{1,2,0:T(8,128)S(1)}, f32[8,64,64]{1,2,0:T(8,128)S(1)}, u32[]{:S(2)}, u32[]{:S(2)}) collective-permute-start(f32[8,64,64]{1,2,0:T(8,128)S(1)} %copy_multiply_fusion), channel_id=1, source_target_pairs={{1,0},{2,1},{3,2},{4,3},{5,4},{6,5},{7,6},{8,7},{9,8},{10,9},{11,1... | collective-permute-start | bytes 393224 | tf_op jit(solution)/shard_map/ppermute | solution.py:17
  15.8 15.4 %collective-permute-start.1 = (f32[8,64,64]{1,2,0:T(8,128)S(1)}, f32[8,64,64]{1,2,0:T(8,128)S(1)}, u32[]{:S(2)}, u32[]{:S(2)}) collective-permute-start(f32[8,64,64]{1,2,0:T(8,128)S(1)} %copy_multiply_fusion), channel_id=1, source_target_pairs={{0,1},{1,2},{2,3},{3,4},{4,5},{5,6},{6,7},{7,8},{8,9},{9,10},{10,1... | collective-permute-start | bytes 393224 | tf_op jit(solution)/shard_map/ppermute | solution.py:17
  18.0 13.2 %collective-permute-start = (f32[8,64,64]{1,2,0:T(8,128)S(1)}, f32[8,64,64]{1,2,0:T(8,128)S(1)}, u32[]{:S(2)}, u32[]{:S(2)}) collective-permute-start(f32[8,64,64]{1,2,0:T(8,128)S(1)} %copy_multiply_fusion), channel_id=1, source_target_pairs={{0,2},{1,3},{2,4},{3,5},{4,6},{5,7},{6,8},{7,9},{8,10},{9,11},{10,... | collective-permute-start | bytes 393224 | tf_op jit(solution)/shard_map/ppermute | solution.py:17
  64.1 13.4 %collective-permute-start.4 = (f32[8,64,64]{1,2,0:T(8,128)S(1)}, f32[8,64,64]{1,2,0:T(8,128)S(1)}, u32[]{:S(2)}, u32[]{:S(2)}) collective-permute-start(f32[8,64,64]{1,2,0:T(8,128)S(1)} %fusion.4), channel_id=1, source_target_pairs={{0,2},{1,3},{2,4},{3,5},{4,6},{5,7},{6,8},{7,9},{8,10},{9,11},{10,... | collective-permute-start | bytes 393224 | tf_op jit(solution)/shard_map/ppermute | solution.py:17
  66.1 13.1 %collective-permute-start.5 = (f32[8,64,64]{1,2,0:T(8,128)S(1)}, f32[8,64,64]{1,2,0:T(8,128)S(1)}, u32[]{:S(2)}, u32[]{:S(2)}) collective-permute-start(f32[8,64,64]{1,2,0:T(8,128)S(1)} %fusion.4), channel_id=1, source_target_pairs={{0,1},{1,2},{2,3},{3,4},{4,5},{5,6},{6,7},{7,8},{8,9},{9,10},{10,1... | collective-permute-start | bytes 393224 | tf_op jit(solution)/shard_map/ppermute | solution.py:17
  68.0 14.7 %collective-permute-start.7 = (f32[8,64,64]{1,2,0:T(8,128)S(1)}, f32[8,64,64]{1,2,0:T(8,128)S(1)}, u32[]{:S(2)}, u32[]{:S(2)}) collective-permute-start(f32[8,64,64]{1,2,0:T(8,128)S(1)} %fusion.4), channel_id=1, source_target_pairs={{2,0},{3,1},{4,2},{5,3},{6,4},{7,5},{8,6},{9,7},{10,8},{11,9},{12,... | collective-permute-start | bytes 393224 | tf_op jit(solution)/shard_map/ppermute | solution.py:17
  74.0 8.6 %collective-permute-start.6 = (f32[8,64,64]{1,2,0:T(8,128)S(1)}, f32[8,64,64]{1,2,0:T(8,128)S(1)}, u32[]{:S(2)}, u32[]{:S(2)}) collective-permute-start(f32[8,64,64]{1,2,0:T(8,128)S(1)} %fusion.4), channel_id=1, source_target_pairs={{1,0},{2,1},{3,2},{4,3},{5,4},{6,5},{7,6},{8,7},{9,8},{10,9},{11,1... | collective-permute-start | bytes 393224 | tf_op jit(solution)/shard_map/ppermute | solution.py:17
